TPU v7x, 256 devices: a whole 4x4x8 slice. The times are simulated.
256 devices in a mesh: ka: 16 (over y, z_hi, core), ga: 16 (over z_lo, x).
Axes of the slice: x: 4, y: 4, z: 8 (z_hi: 2, z_lo: 4; z = z_hi * 4 + z_lo), core: 2. Of those that a mesh axis runs over, the one named last changes fastest.
Arguments:
- bands: bfloat16 [32, 2, 512, 32768], P('ka', None, None, 'ga'), may hold values from -1.5 to 1.5
- nbr_slot: int32 [32], P('ka'), may hold values from 0 to 1, as said below
- gshift: int32 [32], P('ka'), may hold values from -1 to 1
Outputs:
- margin: float32 [512, 32, 2, 512], P('ga', 'ka')
Inputs may be any that keep to these rules, and one draw needn't show every extreme that they name: `nbr_slot`: for the 2 k-points of one group the entries are a permutation of 0 to 1.
All inputs are finite; a program needn't handle non-finite values.
Results may differ from a plain program's by a relative error of at most 0.0028.
Values may be sent and summed in bfloat16 or wider, within the bound.
A program may use at most 128 MiB of HBM per device.

v0:
```python
import math

import jax
import jax.numpy as jnp
from jax import lax
from jax.sharding import PartitionSpec as P

NKB = 4
PLANE = 1024


def shifted(block, axis, distance):
    devices = range(lax.axis_size(axis))
    route = [((i - distance) % len(devices), i) for i in devices]
    return lax.ppermute(block, axis, route)


def phase_fields(slabs, shifts, planes, total_planes):
    turns = (1 + NKB * shifts[:, None]) * planes[None, :] % (NKB * total_planes)
    angle = 2.0 * math.pi / (NKB * total_planes) * turns.astype(jnp.float32)
    cosine = jnp.cos(angle)[:, None, :]
    sine = jnp.sin(angle)[:, None, :]
    real_part = slabs[:, 0].astype(jnp.float32)
    imag_part = slabs[:, 1].astype(jnp.float32)
    near_re = real_part * cosine + imag_part * sine
    near_im = imag_part * cosine - real_part * sine
    return jnp.stack([near_re, near_im], axis=1).astype(jnp.bfloat16)


def body(bands, nbr_slot, gshift):
    grid_index = lax.axis_index("ga")
    grid_count = lax.axis_size("ga")
    nbands = bands.shape[2]
    points = bands.shape[3]
    rows = nbands // grid_count
    total_planes = points // PLANE * grid_count
    planes = (grid_index * points + jnp.arange(points, dtype=jnp.int32)) // PLANE
    there = shifted(bands, "ka", -1)
    partner = jnp.take(there, nbr_slot, axis=0)
    near = phase_fields(partner, gshift, planes, total_planes)
    terms = jnp.einsum("pcmx,pdnx->mpcdn", bands, near, preferred_element_type=jnp.float32)
    real_part = terms[:, :, 0, 0] + terms[:, :, 1, 1]
    imag_part = terms[:, :, 0, 1] - terms[:, :, 1, 0]
    summed = lax.psum(jnp.stack([real_part, imag_part], axis=2), "ga")
    result = lax.dynamic_slice_in_dim(summed, grid_index * rows, rows, 0)
    return result


def solution(mesh):
    placed = (P("ka", None, None, "ga"), P("ka"), P("ka"))
    return jax.shard_map(
        body, mesh=mesh, in_specs=placed, out_specs=P("ga", "ka", None, None), check_vma=False
    )
```

profile of v0, /device:TPU:1, one launch (start us, length us, event | category | flops | bytes accessed | tf_op | source)
XLA Modules:
  0.0 421.2 jit_solution(4807818355524482640)
XLA Ops:
  6.5 0.0 all-reduce.2.cloned.1.call-start
  6.5 3.2 collective-permute-start
  9.8 0.7 compare_select_fusion.2
  10.5 0.7 compare_and_fusion
  11.1 0.7 multiply_add_fusion
  11.8 0.3 fusion.20
  12.1 153.4 %collective-permute-done = bf16[2,2,512,2048]{3,2,1,0:T(8,128)(2,1)} collective-permute-done((bf16[2,2,512,2048]{3,2,1,0:T(8,128)(2,1)}, bf16[2,2,512,2048]{3,2,1,0:T(8,128)(2,1)}, u32[]{:S(2)}, u32[]{:S(2)}) %collective-permute-start) | collective-permute-done | bytes 8388640 | tf_op jit(solution)/shard_map/ppermute | solution.py:15
  165.6 1.7 mini-gather-slice.5
  167.3 2.0 gather_fusion.2
  169.3 6.0 %fusion.23 = (bf16[2,2,512,768]{3,2,1,0:T(8,128)(2,1)}, bf16[2,2,512,768]{3,2,1,0:T(8,128)(2,1)}) fusion(bf16[2,2,512,2048]{3,2,1,0:T(8,128)(2,1)} %collective-permute-done), kind=kLoop, calls=%fused_computation.49 | loop fusion | bytes 12582912 | tf_op jit(solution)/shard_map/jit(_take)/gather | solution.py:39
  175.2 2.6 gather_fusion.1
  177.9 4.3 %gather_fusion = bf16[2,2,512,768]{3,2,1,0:T(8,128)(2,1)} fusion(bf16[2,2,512,768]{3,2,1,0:T(8,128)(2,1)} %get-tuple-element.7, s32[1024]{0:T(1024)S(1)} %pad_clamp_fusion), kind=kCustom, calls=%fused_computation | custom fusion | bytes 6291464 | tf_op jit(solution)/shard_map/jit(_take)/gather | solution.py:39
  182.2 4.4 %maximum_select_fusion = bf16[2,2,512,2048]{3,2,1,0:T(8,128)(2,1)S(1)} fusion(bf16[2,2,512,512]{3,2,1,0:T(8,128)(2,1)} %gather_fusion.2, bf16[2,2,512,768]{3,2,1,0:T(8,128)(2,1)S(1)} %gather_fusion.1, bf16[2,2,512,768]{3,2,1,0:T(8,128)(2,1)} %gather_fusion, pred[2]{0:T(512)(128)(4,1)S(1)} %compare_and_fusion), kind=kLoop, calls=%fused_computation.11 | loop fusion | flops 29360128 | bytes 16777218 | tf_op jit(solution)/shard_map/jit(_take)/select_n | solution.py:39
  186.5 5.1 %fusion.1 = (bf16[2,1,512,2048]{3,2,1,0:T(8,128)(2,1)}, bf16[2,1,512,2048]{3,2,1,0:T(8,128)(2,1)}) fusion(f32[2,2048]{1,0:T(2,128)S(1)} %get-tuple-element.10, f32[2,2048]{1,0:T(2,128)S(1)} %get-tuple-element.9, bf16[2,2,512,2048]{3,2,1,0:T(8,128)(2,1)S(1)} %maximum_select_fusion), kind=kLoop, calls=%fused_computation.8 | loop fusion | flops 20971520 | bytes 16809984 | tf_op jit(solution)/shard_map/convert
  191.6 12.6 %fusion.8 = f32[512,2,2,2,512]{0,4,2,3,1:T(8,128)S(1)} fusion(bf16[2,2,512,2048]{3,2,1,0:T(8,128)(2,1)} %param.3, bf16[2,1,512,2048]{3,2,1,0:T(8,128)(2,1)} %get-tuple-element.6, bf16[2,1,512,2048]{3,2,1,0:T(8,128)(2,1)} %get-tuple-element.5), kind=kOutput, calls=%fused_computation.18 | convolution fusion | flops 8606711808 | bytes 25165824 | tf_op jit(solution)/shard_map/pcmx,pdnx->mpcdn/dot_general | solution.py:41
  204.2 0.5 fusion.11
  204.6 0.5 fusion.13
  205.1 2.4 pad_maximum_fusion
  207.5 0.0 all-reduce.2.cloned.1.call-update
  207.6 204.2 %all-reduce.2.cloned.1.call-done = f32[512,2,2,512]{0,3,1,2:T(8,128)} async-done(((f32[512,2,2,512]{0,3,1,2:T(8,128)}), f32[512,2,2,512]{0,3,1,2:T(8,128)}) %all-reduce.2.cloned.1.call-update) | async-done | bytes 4194320 | tf_op jit(solution)/shard_map/psum | solution.py:44
  411.8 1.6 constant_dynamic-slice_fusion
  413.3 1.0 copy.6
  (2 shorter events, 0.0 us)
Async XLA Ops:
  6.5 405.2 %all-reduce.2.cloned.1.call-start = ((), (), s32[]{:S(2)}) async-start(), calls=%async_computation | async-start | bytes 8388608 | tf_op jit(solution)/shard_map/psum | solution.py:44
  6.5 159.0 %collective-permute-start = (bf16[2,2,512,2048]{3,2,1,0:T(8,128)(2,1)}, bf16[2,2,512,2048]{3,2,1,0:T(8,128)(2,1)}, u32[]{:S(2)}, u32[]{:S(2)}) collective-permute-start(bf16[2,2,512,2048]{3,2,1,0:T(8,128)(2,1)} %param.3), channel_id=1, source_target_pairs={{16,0},{32,16},{48,32},{64,48},{80,64},{96,80},{112,96},{128,112},... | collective-permute-start | bytes 25165832 | tf_op jit(solution)/shard_map/ppermute | solution.py:15
Sparse Core Ops, SparseCore 0:
  207.7 204.0 all-reduce.1
where the time goes:
time: 429 us; the launch traced here: 421 us
  waiting for transfers between devices  358 us (83%)
  local copies, waits for them, and re-layouts  19.2 us (4%)
  other arithmetic  15.1 us (4%)
  between operations  13.4 us (3%)
  matrix products  12.6 us (3%)
    psum x1, waiting for transfers between devices, body(): summed = lax.psum(jnp.stack([real_part, imag_part], axis=2), 'ga')  204 us
    ppermute x1, waiting for transfers between devices, shifted(): return lax.ppermute(block, axis, route)  153 us
    gather x5, local copies, waits for them, and re-layouts, body(): partner = jnp.take(there, nbr_slot, axis=0)  16.6 us
    dot_general x1, matrix products, body(): jnp.einsum('pcmx,pdnx->mpcdn', bands, near, preferred_element_type=jnp.fl...  12.6 us
  transfers between devices with their start and end apart: 2, of which 2 were waited for; matrix products, arithmetic and copies ran while one was open for 1% of the time, Pallas kernels for 0%

commit v1 on v0

v1 whole, which is shorter than its diff:
```python
import math

import jax
import jax.numpy as jnp
from jax import lax
from jax.experimental import pallas as pl
from jax.experimental.pallas import tpu as pltpu
from jax.sharding import PartitionSpec as P

NKB = 4
PLANE = 1024
NX_DEV = 4
CHUNKS = 8
MESH = pl.DeviceIdType.MESH


def kernel(
    slot_ref, shift_ref, bands, out_ref,
    own, there, trig, near, part, xbuf, zsend, zbuf, result,
    own_sem, send_sem, recv_sem, xsend_sem, xrecv_sem, zsend_sem, zrecv_sem,
):
    ka, ga = lax.axis_index("ka"), lax.axis_index("ga")
    n_ka, n_ga = lax.axis_size("ka"), lax.axis_size("ga")
    n_x = NX_DEV
    n_z = n_ga // n_x
    z, x = ga // n_x, lax.rem(ga, n_x)
    chunks, cols = there.shape[0], there.shape[3]
    kpts, points = there.shape[1], there.shape[4]
    rows = out_ref.shape[2]
    total_planes = points // PLANE * n_ga

    before = lax.rem(ka + n_ka - 1, n_ka)
    after = lax.rem(ka + 1, n_ka)

    def along_x(d):
        return z * n_x + lax.rem(x + d + n_x, n_x)

    def along_z(d):
        return lax.rem(z + d + n_z, n_z) * n_x + x

    fetch = pltpu.make_async_copy(bands, own, own_sem)
    fetch.start()

    barrier = pltpu.get_barrier_semaphore()
    greeted = [(before, ga), (after, ga)]
    greeted += [(ka, along_x(d)) for d in range(1, n_x)]
    greeted += [(ka, along_z(d)) for d in range(1, n_z)]
    for device in greeted:
        pl.semaphore_signal(barrier, inc=1, device_id=device, device_id_type=MESH)
    pl.semaphore_wait(barrier, len(greeted))

    def slab_copy(c):
        return pltpu.make_async_remote_copy(
            src_ref=bands.at[:, :, pl.ds(c * cols, cols), :],
            dst_ref=there.at[c],
            send_sem=send_sem.at[c],
            recv_sem=recv_sem.at[c],
            device_id=(before, ga),
            device_id_type=MESH,
        )

    def x_copy(c, d):
        return pltpu.make_async_remote_copy(
            src_ref=part.at[c, :, :, lax.rem(x + d, n_x)],
            dst_ref=xbuf.at[c, d - 1],
            send_sem=xsend_sem.at[c, d - 1],
            recv_sem=xrecv_sem.at[c, d - 1],
            device_id=(ka, along_x(d)),
            device_id_type=MESH,
        )

    def z_copy(c, d):
        return pltpu.make_async_remote_copy(
            src_ref=zsend.at[c, d - 1],
            dst_ref=zbuf.at[c, d - 1],
            send_sem=zsend_sem.at[c, d - 1],
            recv_sem=zrecv_sem.at[c, d - 1],
            device_id=(ka, along_z(d)),
            device_id_type=MESH,
        )

    @pl.loop(0, chunks)
    def _(c):
        slab_copy(c).start()

    plane = ga * (points // PLANE) + lax.broadcasted_iota(jnp.int32, (1, points), 1) // PLANE
    for k in range(kpts):
        turns = (1 + NKB * shift_ref[k]) * plane % (NKB * total_planes)
        angle = 2.0 * math.pi / (NKB * total_planes) * turns.astype(jnp.float32)
        trig[k, 0:1] = jnp.cos(angle)
        trig[k, 1:2] = jnp.sin(angle)

    fetch.wait()

    def multiply(c):
        slab_copy(c).wait_recv()

        @pl.loop(0, cols // 16)
        def _(step):
            lo = pl.multiple_of(step * 16, 16)
            for k in range(kpts):
                first = slot_ref[k] == 0
                re = jnp.where(first, there[c, 0, 0, pl.ds(lo, 16), :], there[c, 1, 0, pl.ds(lo, 16), :]).astype(jnp.float32)
                im = jnp.where(first, there[c, 0, 1, pl.ds(lo, 16), :], there[c, 1, 1, pl.ds(lo, 16), :]).astype(jnp.float32)
                cosine, sine = trig[k, 0:1], trig[k, 1:2]
                near_re = (re * cosine + im * sine).astype(jnp.bfloat16)
                near_im = (im * cosine - re * sine).astype(jnp.bfloat16)
                near[k, 0, pl.ds(lo, 16), :] = near_re
                near[k, 0, pl.ds(cols + lo, 16), :] = near_im
                near[k, 1, pl.ds(lo, 16), :] = near_im
                near[k, 1, pl.ds(cols + lo, 16), :] = -near_re

        @pl.loop(0, kpts)
        def _(k):
            over_points = (((1,), (1,)), ((), ()))
            terms = lax.dot_general(own[k, 0], near[k, 0], over_points, preferred_element_type=jnp.float32)
            terms += lax.dot_general(own[k, 1], near[k, 1], over_points, preferred_element_type=jnp.float32)
            part[c, k] = terms.reshape(part.shape[2:])

        for d in range(1, n_x):
            x_copy(c, d).start()

    def sum_x(c):
        for d in range(1, n_x):
            x_copy(c, d).wait_recv()

        def at(zz):
            total = part[c, :, zz, x]
            for d in range(1, n_x):
                total += xbuf[c, d - 1, :, zz]
            return total

        for d in range(1, n_z):
            zsend[c, d - 1] = at(lax.rem(z + d, n_z)).astype(jnp.bfloat16)
            z_copy(c, d).start()
        result[c] = at(z)

    def sum_z(c):
        for d in range(1, n_z):
            z_copy(c, d).wait_recv()
        total = result[c]
        for d in range(1, n_z):
            total += zbuf[c, d - 1].astype(jnp.float32)
        result[c] = total

    @pl.loop(0, chunks)
    def _(c):
        multiply(c)

        @pl.when(c >= 1)
        def _():
            sum_x(c - 1)

        @pl.when(c >= 2)
        def _():
            sum_z(c - 2)

    sum_x(chunks - 1)
    sum_z(chunks - 2)
    sum_z(chunks - 1)

    for k in range(kpts):
        for half in range(2):
            pieces = [result[c, k][:, half * cols : (half + 1) * cols] for c in range(chunks)]
            out_ref[k, half] = jnp.concatenate(pieces, axis=1)

    @pl.loop(0, chunks)
    def _(c):
        slab_copy(c).wait_send()
        for d in range(1, n_x):
            x_copy(c, d).wait_send()
        for d in range(1, n_z):
            z_copy(c, d).wait_send()


def body(bands, nbr_slot, gshift):
    kpts, _, nbands, points = bands.shape
    n_x = NX_DEV
    n_ga = lax.axis_size("ga")
    n_z = n_ga // n_x
    rows = nbands // n_ga
    cols = nbands // CHUNKS
    out = pl.pallas_call(
        kernel,
        name="margins",
        out_shape=jax.ShapeDtypeStruct((kpts, 2, rows, nbands), jnp.float32),
        in_specs=[
            pl.BlockSpec(memory_space=pltpu.SMEM),
            pl.BlockSpec(memory_space=pltpu.SMEM),
            pl.BlockSpec(memory_space=pl.ANY),
        ],
        out_specs=pl.BlockSpec(memory_space=pltpu.VMEM),
        scratch_shapes=[
            pltpu.VMEM((kpts, 2, nbands, points), jnp.bfloat16),
            pltpu.VMEM((CHUNKS, kpts, 2, cols, points), jnp.bfloat16),
            pltpu.VMEM((kpts, 2, points), jnp.float32),
            pltpu.VMEM((kpts, 2, 2 * cols, points), jnp.bfloat16),
            pltpu.VMEM((CHUNKS, kpts, n_z, n_x, rows, 2 * cols), jnp.float32),
            pltpu.VMEM((CHUNKS, n_x - 1, kpts, n_z, rows, 2 * cols), jnp.float32),
            pltpu.VMEM((CHUNKS, n_z - 1, kpts, rows, 2 * cols), jnp.bfloat16),
            pltpu.VMEM((CHUNKS, n_z - 1, kpts, rows, 2 * cols), jnp.bfloat16),
            pltpu.VMEM((CHUNKS, kpts, rows, 2 * cols), jnp.float32),
            pltpu.SemaphoreType.DMA,
            pltpu.SemaphoreType.DMA((CHUNKS,)),
            pltpu.SemaphoreType.DMA((CHUNKS,)),
            pltpu.SemaphoreType.DMA((CHUNKS, n_x - 1)),
            pltpu.SemaphoreType.DMA((CHUNKS, n_x - 1)),
            pltpu.SemaphoreType.DMA((CHUNKS, n_z - 1)),
            pltpu.SemaphoreType.DMA((CHUNKS, n_z - 1)),
        ],
        compiler_params=pltpu.CompilerParams(
            collective_id=0, has_side_effects=True, vmem_limit_bytes=48 * 1024 * 1024
        ),
    )(nbr_slot, gshift, bands)
    return jnp.transpose(out, (2, 0, 1, 3))


def solution(mesh):
    placed = (P("ka", None, None, "ga"), P("ka"), P("ka"))
    return jax.shard_map(
        body, mesh=mesh, in_specs=placed, out_specs=P("ga", "ka", None, None), check_vma=False
    )
```

time: 429 us -> 236 us (0.55); the launches traced: 421 us -> 236 us
  waiting for transfers between devices: 358 us -> 0 us
  Pallas kernels: 0 us -> 233 us
  local copies, waits for them, and re-layouts: 19.2 us -> 2.22 us
  other arithmetic: 15.1 us -> 0 us
  between operations: 13.4 us -> 0.01 us
  matrix products: 12.6 us -> 0 us
    pallas_call x0 -> x1, Pallas kernels: none -> 233 us  [body(): pl.pallas_call(kernel, name='margins', out_shape=jax.ShapeDtypeStruct((kp...]
    psum x1 -> x0, waiting for transfers between devices: 204 us -> none  [body(): summed = lax.psum(jnp.stack([real_part, imag_part], axis=2), 'ga')]
    ppermute x1 -> x0, waiting for transfers between devices: 153 us -> none  [shifted(): return lax.ppermute(block, axis, route)]
    gather x5 -> x0, local copies, waits for them, and re-layouts: 16.6 us -> none  [body(): partner = jnp.take(there, nbr_slot, axis=0)]
    dot_general x1 -> x0, matrix products: 12.6 us -> none  [body(): jnp.einsum('pcmx,pdnx->mpcdn', bands, near, preferred_element_type=jnp.fl...]
    another operation x2 -> x0, other arithmetic: 7.46 us -> none
    select_n x3 -> x0, other arithmetic: 5.03 us -> none  [the longest x2 5.02 us: body(): partner = jnp.take(there, nbr_slot, axis=0)]
  transfers between devices with their start and end apart: 2 -> 0, of which waited for: 2 -> 0; matrix products, arithmetic and copies ran while one was open for 1% -> 0% of each run, Pallas kernels for 0% -> 0%
where the time goes in v1:
time: 236 us
  Pallas kernels  233 us (99%)
    pallas_call x1, Pallas kernels, body(): pl.pallas_call(kernel, name='margins', out_shape=jax.ShapeDtypeStruct((kp...  233 us

profile of v1, /device:TPU:1, one launch (start us, length us, event | category | flops | bytes accessed | tf_op | source)
XLA Modules:
  0.0 235.7 jit_solution(10740317451835582492)
XLA Ops:
  0.0 0.0 copy-start
  0.0 0.7 copy-done
  0.7 0.0 copy-start.1
  0.7 0.7 copy-done.1
  1.3 233.5 %margins.1 = f32[2,2,32,512]{3,2,1,0:T(8,128)S(1)} custom-call(s32[2]{0:T(128)S(1)} %copy-done, s32[2]{0:T(128)S(1)} %copy-done.1, bf16[2,2,512,2048]{3,2,1,0:T(8,128)(2,1)} %bands.1), custom_call_target="tpu_custom_call" | custom-call | tf_op jit(solution)/shard_map/margins/pallas_call | solution.py:183
  234.8 0.9 copy.4
Async XLA Ops:
  0.0 0.7 copy-start
  0.7 0.7 copy-start.1

commit v2 on v0

v2 whole, which is shorter than its diff:
```python
import contextlib
import math

import jax
import jax.numpy as jnp
from jax import lax
from jax.experimental import pallas as pl
from jax.experimental.pallas import tpu as pltpu
from jax.sharding import PartitionSpec as P

NKB = 4
PLANE = 1024
N_X = 4
CHUNKS = 16
DEPTH = 3
TILE = 16
LANES = 128
LAG = 3
MESH = pl.DeviceIdType.MESH
OVER_POINTS = (((1,), (1,)), ((), ()))


def scope(name):
    return contextlib.nullcontext()


def kernel(
    slot_hbm, shift_hbm, bands, out_ref,
    slot_ref, shift_ref, own, there, trig, near, part, xbuf, zsend, zmid, zbuf, last_send, last_buf, result,
    own_sem, small_sem, pace_sem, core_sem, recv_sem, xsend_sem, xrecv_sem, zsend_sem, zmid_sem, zrecv_sem,
    last_send_sem, last_recv_sem,
):
    ka, ga = lax.axis_index("ka"), lax.axis_index("ga")
    n_ka, n_ga = lax.axis_size("ka"), lax.axis_size("ga")
    n_x = N_X
    n_z = n_ga // n_x
    z, x = ga // n_x, lax.rem(ga, n_x)
    core = lax.rem(ka, 2)
    pieces, kpts, _, cols, _ = there.shape
    chunks = part.shape[0]
    halves = pieces // chunks
    points = own.shape[3]
    total_planes = points // PLANE * n_ga

    before = lax.rem(ka + n_ka - 1, n_ka)
    after = lax.rem(ka + 1, n_ka)

    others = [(dz, dx) for dz in range(n_z) for dx in range(n_x) if dz or dx]

    def relative(dz, dx):
        return lax.rem(z + dz, n_z) * n_x + lax.rem(x + dx, n_x)

    fetch = pltpu.make_async_copy(bands, own, own_sem)
    fetch.start()
    small = [
        pltpu.make_async_copy(slot_hbm, slot_ref, small_sem.at[0]),
        pltpu.make_async_copy(shift_hbm, shift_ref, small_sem.at[1]),
    ]
    for copy in small:
        copy.start()

    barrier = pltpu.get_barrier_semaphore()
    greeted = [(before, ga), (after, ga)]
    greeted += [(ka, relative(*away)) for away in others]
    for device in greeted:
        pl.semaphore_signal(barrier, inc=1, device_id=device, device_id_type=MESH)
    with scope("barrier"):
        pl.semaphore_wait(barrier, len(greeted))

    def slab_copy(p, sem):
        c, h = p // halves, lax.rem(p, halves)
        rows = pl.ds(pl.multiple_of(c * cols, cols), cols)
        lanes = pl.ds(pl.multiple_of(h * PLANE, PLANE), PLANE)
        return pltpu.make_async_remote_copy(
            src_ref=bands.at[:, :, rows, lanes],
            dst_ref=there.at[p],
            send_sem=sem,
            recv_sem=recv_sem.at[p],
            device_id=(before, ga),
            device_id_type=MESH,
        )

    def x_copy(c, d):
        return pltpu.make_async_remote_copy(
            src_ref=part.at[c, :, lax.rem(x + d, n_x)],
            dst_ref=xbuf.at[c, d - 1],
            send_sem=xsend_sem,
            recv_sem=xrecv_sem.at[c],
            device_id=(ka, relative(0, d)),
            device_id_type=MESH,
        )

    inward = jnp.where(z < n_z // 2, 1, -1)
    outer = (z == 0) | (z == n_z - 1)

    def to_inner(c):
        return pltpu.make_async_remote_copy(
            src_ref=zsend.at[c],
            dst_ref=zmid.at[c],
            send_sem=zsend_sem,
            recv_sem=zmid_sem.at[c],
            device_id=(ka, ga + inward * n_x),
            device_id_type=MESH,
        )

    def from_inner(c, j):
        far = (-1, 1, 2)[j]
        return pltpu.make_async_remote_copy(
            src_ref=zsend.at[c, j],
            dst_ref=zbuf.at[c, 0 if j else 1],
            send_sem=zsend_sem,
            recv_sem=zrecv_sem.at[c],
            device_id=(ka, ga + far * inward * n_x),
            device_id_type=MESH,
        )

    def last_copy(dz, dx):
        return pltpu.make_async_remote_copy(
            src_ref=last_send.at[lax.rem(z + dz, n_z), lax.rem(x + dx, n_x)],
            dst_ref=last_buf.at[dz * n_x + dx],
            send_sem=last_send_sem,
            recv_sem=last_recv_sem,
            device_id=(ka, relative(dz, dx)),
            device_id_type=MESH,
        )

    def wait_for(ref, sem):
        pltpu.make_async_copy(ref, ref, sem).wait()

    @pl.when(core == 1)
    def _():
        @pl.loop(0, pieces)
        def _(p):
            slab_copy(p, core_sem).start()

    @pl.when(core == 0)
    def _():
        @pl.loop(0, DEPTH)
        def _(p):
            slab_copy(p, pace_sem.at[p]).start()

    for copy in small:
        copy.wait()
    plane = ga * (points // PLANE) + lax.broadcasted_iota(jnp.int32, (1, points), 1) // PLANE
    for k in range(kpts):
        turns = (1 + NKB * shift_ref[k]) * plane % (NKB * total_planes)
        angle = 2.0 * math.pi / (NKB * total_planes) * turns.astype(jnp.float32)
        trig[k, 0:1] = jnp.cos(angle)
        trig[k, 1:2] = jnp.sin(angle)

    near[...] = jnp.zeros_like(near)

    fetch.wait()

    def multiply(p):
        c, h = p // halves, lax.rem(p, halves)
        lanes = pl.ds(pl.multiple_of(h * PLANE, PLANE), PLANE)
        with scope("slab"):
            wait_for(there.at[p], recv_sem.at[p])

        @pl.loop(0, cols // TILE)
        def _(step):
            lo = pl.multiple_of(step * TILE, TILE)
            rows = pl.ds(lo, TILE)
            re_0, im_0, re_1, im_1 = (there[p, k, part_, rows, :] for k in range(kpts) for part_ in range(2))
            for k in range(kpts):
                first = slot_ref[k] == 0
                re = jnp.where(first, re_0, re_1).astype(jnp.float32)
                im = jnp.where(first, im_0, im_1).astype(jnp.float32)
                cosine, sine = trig[k, 0:1, lanes], trig[k, 1:2, lanes]
                near_re = (re * cosine + im * sine).astype(jnp.bfloat16)
                near_im = (im * cosine - re * sine).astype(jnp.bfloat16)
                upper = pl.ds(2 * k * cols + lo, TILE)
                lower = pl.ds((2 * k + 1) * cols + lo, TILE)
                near[k, 0, upper, :] = near_re
                near[k, 0, lower, :] = near_im
                near[k, 1, upper, :] = near_im
                near[k, 1, lower, :] = -near_re

        terms = None
        for k in range(kpts):
            for half in range(2):
                term = lax.dot_general(
                    own[k, half, :, lanes], near[k, half], OVER_POINTS, preferred_element_type=jnp.float32
                )
                terms = term if terms is None else terms + term
        terms = terms.reshape(part.shape[1:])

        @pl.when(h == 0)
        def _():
            part[c] = terms

        @pl.when(h > 0)
        def _():
            part[c] += terms

        @pl.when((h == halves - 1) & (c < chunks - 1))
        def _():
            for d in range(1, n_x):
                x_copy(c, d).start()

        @pl.when((h == halves - 1) & (c == chunks - 1))
        def _():
            last_send[...] = part[c].astype(jnp.bfloat16)
            for away in others:
                last_copy(*away).start()

    def over_x(c, zz):
        total = part[c, zz, x]
        for d in range(1, n_x):
            total += xbuf[c, d - 1, zz]
        return total

    def sum_x(c):
        with scope("sumx"):
            wait_for(xbuf.at[c], xrecv_sem.at[c])

        @pl.when(outer)
        def _():
            for j in range(n_z - 1):
                zsend[c, j] = over_x(c, z + (j + 1) * inward).astype(jnp.bfloat16)
            to_inner(c).start()

        @pl.when(jnp.logical_not(outer))
        def _():
            zsend[c, 0] = over_x(c, z - inward).astype(jnp.bfloat16)
            from_inner(c, 0).start()

        result[c] = over_x(c, z)

    def sum_inner(c):
        @pl.when(jnp.logical_not(outer))
        def _():
            with scope("inner"):
                wait_for(zmid.at[c], zmid_sem.at[c])
            for j in (1, 2):
                total = over_x(c, z + j * inward) + zmid[c, j].astype(jnp.float32)
                zsend[c, j] = total.astype(jnp.bfloat16)
                from_inner(c, j).start()
            result[c] += zmid[c, 0].astype(jnp.float32)

    def sum_z(c):
        @pl.when(outer)
        def _():
            with scope("sumz"):
                wait_for(zbuf.at[c], zrecv_sem.at[c])
            result[c] += zbuf[c, 0].astype(jnp.float32) + zbuf[c, 1].astype(jnp.float32)

        @pl.when(jnp.logical_not(outer))
        def _():
            with scope("sumz"):
                wait_for(zbuf.at[c, 0], zrecv_sem.at[c])
            result[c] += zbuf[c, 0].astype(jnp.float32)

    @pl.loop(0, pieces)
    def _(i):
        @pl.when((core == 0) & (i >= DEPTH))
        def _():
            sem = pace_sem.at[lax.rem(i, DEPTH)]
            with scope("pace"):
                wait_for(there.at[i], sem)
            slab_copy(i, sem).start()

        first = jnp.where(core == 0, jnp.minimum(halves * i, pieces), i)
        last = jnp.where(core == 0, jnp.minimum(halves * i + halves, pieces), i + 1)

        @pl.loop(first, last)
        def _(p):
            multiply(p)

        whole = (core == 0) | (lax.rem(i, halves) == halves - 1)
        c = jnp.where(core == 0, i, i // halves)
        lag = jnp.where(core == 0, 2 * LAG, LAG)

        @pl.when(whole & (c >= 1) & (c < chunks))
        def _():
            sum_x(c - 1)

        @pl.when(whole & (c > lag) & (c - lag < chunks))
        def _():
            sum_inner(c - lag - 1)

    @pl.loop(jnp.where(core == 0, chunks - 1, chunks - LAG - 1), chunks - 1)
    def _(c):
        sum_inner(c)

    @pl.loop(0, chunks - 1)
    def _(c):
        sum_z(c)

    with scope("last"):
        wait_for(last_buf.at[pl.ds(1, n_z * n_x - 1)], last_recv_sem)
    total = part[chunks - 1, z, x]
    for dz, dx in others:
        total += last_buf[dz * n_x + dx].astype(jnp.float32)
    result[chunks - 1] = total

    blocks = chunks * cols // LANES
    rows = result.shape[1]
    for k in range(kpts):
        for half in range(2):
            lo = (2 * k + half) * cols
            for b in range(blocks):
                members = range(b * chunks // blocks, (b + 1) * chunks // blocks)
                block = jnp.concatenate([result[c][:, lo : lo + cols] for c in members], axis=1)
                out_ref[pl.ds((k * blocks + b) * 2 + half, rows, stride=kpts * blocks * 2), :] = block

    with scope("end"):
        @pl.when(core == 1)
        def _():
            wait_for(there, core_sem)

        @pl.when(core == 0)
        def _():
            @pl.loop(0, DEPTH)
            def _(p):
                wait_for(there.at[p], pace_sem.at[p])

        wait_for(xbuf, xsend_sem)
        wait_for(zsend, zsend_sem)
        wait_for(last_buf.at[pl.ds(1, n_z * n_x - 1)], last_send_sem)


def body(bands, nbr_slot, gshift):
    kpts, _, nbands, points = bands.shape
    n_x = N_X
    n_ga = lax.axis_size("ga")
    n_z = n_ga // n_x
    rows = nbands // n_ga
    cols = nbands // CHUNKS
    lanes = 2 * kpts * cols
    pieces = CHUNKS * (points // PLANE)
    out = pl.pallas_call(
        kernel,
        name="margins",
        out_shape=jax.ShapeDtypeStruct((rows * kpts * 2 * nbands // LANES, LANES), jnp.float32),
        in_specs=[
            pl.BlockSpec(memory_space=pltpu.HBM),
            pl.BlockSpec(memory_space=pltpu.HBM),
            pl.BlockSpec(memory_space=pl.ANY),
        ],
        out_specs=pl.BlockSpec(memory_space=pltpu.VMEM),
        scratch_shapes=[
            pltpu.SMEM((kpts,), jnp.int32),
            pltpu.SMEM((kpts,), jnp.int32),
            pltpu.VMEM((kpts, 2, nbands, points), jnp.bfloat16),
            pltpu.VMEM((pieces, kpts, 2, cols, PLANE), jnp.bfloat16),
            pltpu.VMEM((kpts, 2, points), jnp.float32),
            pltpu.VMEM((kpts, 2, lanes, PLANE), jnp.bfloat16),
            pltpu.VMEM((CHUNKS, n_z, n_x, rows, lanes), jnp.float32),
            pltpu.VMEM((CHUNKS - 1, n_x - 1, n_z, rows, lanes), jnp.float32),
            pltpu.VMEM((CHUNKS - 1, n_z - 1, rows, lanes), jnp.bfloat16),
            pltpu.VMEM((CHUNKS - 1, n_z - 1, rows, lanes), jnp.bfloat16),
            pltpu.VMEM((CHUNKS - 1, 2, rows, lanes), jnp.bfloat16),
            pltpu.VMEM((n_z, n_x, rows, lanes), jnp.bfloat16),
            pltpu.VMEM((n_z * n_x, rows, lanes), jnp.bfloat16),
            pltpu.VMEM((CHUNKS, rows, lanes), jnp.float32),
            pltpu.SemaphoreType.DMA,
            pltpu.SemaphoreType.DMA((2,)),
            pltpu.SemaphoreType.DMA((DEPTH,)),
            pltpu.SemaphoreType.DMA,
            pltpu.SemaphoreType.DMA((pieces,)),
            pltpu.SemaphoreType.DMA,
            pltpu.SemaphoreType.DMA((CHUNKS - 1,)),
            pltpu.SemaphoreType.DMA,
            pltpu.SemaphoreType.DMA((CHUNKS - 1,)),
            pltpu.SemaphoreType.DMA((CHUNKS - 1,)),
            pltpu.SemaphoreType.DMA,
            pltpu.SemaphoreType.DMA,
        ],
        compiler_params=pltpu.CompilerParams(
            collective_id=0, has_side_effects=True, vmem_limit_bytes=63 * 1024 * 1024
        ),
    )(nbr_slot, gshift, bands)
    out = out.reshape(rows, kpts, nbands // LANES, 2, LANES)
    return jnp.transpose(out, (0, 1, 3, 2, 4)).reshape(rows, kpts, 2, nbands)


def solution(mesh):
    placed = (P("ka", None, None, "ga"), P("ka"), P("ka"))
    return jax.shard_map(
        body, mesh=mesh, in_specs=placed, out_specs=P("ga", "ka", None, None), check_vma=False
    )
```

time: 429 us -> 213 us (0.50); the launches traced: 421 us -> 211 us
  waiting for transfers between devices: 358 us -> 0 us
  Pallas kernels: 0 us -> 210 us
  local copies, waits for them, and re-layouts: 19.2 us -> 1.67 us
  other arithmetic: 15.1 us -> 0 us
  between operations: 13.4 us -> 0.01 us
  matrix products: 12.6 us -> 0 us
    pallas_call x0 -> x1, Pallas kernels: none -> 210 us  [body(): pl.pallas_call(kernel, name='margins', out_shape=jax.ShapeDtypeStruct((ro...]
    psum x1 -> x0, waiting for transfers between devices: 204 us -> none  [body(): summed = lax.psum(jnp.stack([real_part, imag_part], axis=2), 'ga')]
    ppermute x1 -> x0, waiting for transfers between devices: 153 us -> none  [shifted(): return lax.ppermute(block, axis, route)]
    gather x5 -> x0, local copies, waits for them, and re-layouts: 16.6 us -> none  [body(): partner = jnp.take(there, nbr_slot, axis=0)]
    dot_general x1 -> x0, matrix products: 12.6 us -> none  [body(): jnp.einsum('pcmx,pdnx->mpcdn', bands, near, preferred_element_type=jnp.fl...]
    another operation x2 -> x0, other arithmetic: 7.46 us -> none
    select_n x3 -> x0, other arithmetic: 5.03 us -> none  [the longest x2 5.02 us: body(): partner = jnp.take(there, nbr_slot, axis=0)]
  transfers between devices with their start and end apart: 2 -> 0, of which waited for: 2 -> 0; matrix products, arithmetic and copies ran while one was open for 1% -> 0% of each run, Pallas kernels for 0% -> 0%
where the time goes in v2:
time: 213 us; the launch traced here: 211 us
  Pallas kernels  210 us (99%)
    pallas_call x1, Pallas kernels, body(): pl.pallas_call(kernel, name='margins', out_shape=jax.ShapeDtypeStruct((ro...  210 us

profile of v2, /device:TPU:1, one launch (start us, length us, event | category | flops | bytes accessed | tf_op | source)
XLA Modules:
  0.0 211.3 jit_solution(7390623686887095091)
XLA Ops:
  0.0 209.6 %margins.1 = f32[512,128]{1,0:T(8,128)} custom-call(s32[2]{0:T(128)} %slot_hbm.1, s32[2]{0:T(128)} %shift_hbm.1, bf16[2,2,512,2048]{3,2,1,0:T(8,128)(2,1)} %bands.1), custom_call_target="tpu_custom_call" | custom-call | tf_op jit(solution)/shard_map/margins/pallas_call | solution.py:333
  209.6 1.7 copy.6

commit v3 on v2

--- a/solution.py
+++ b/solution.py
@@ -268,7 +268,7 @@
         def _(p):
             multiply(p)
 
-        whole = (core == 0) | (lax.rem(i, halves) == halves - 1)
+        whole = (core == 0) | (lax.rem(i, halves) == 0)
         c = jnp.where(core == 0, i, i // halves)
         lag = jnp.where(core == 0, 2 * LAG, LAG)
 

time: 213 us -> 215 us (level)
  no operation moved by 1% of the time
where the time goes in v3:
time: 215 us; the launch traced here: 212 us
  Pallas kernels  211 us (98%)
    pallas_call x1, Pallas kernels, body(): pl.pallas_call(kernel, name='margins', out_shape=jax.ShapeDtypeStruct((ro...  211 us

profile of v3, /device:TPU:1, one launch (start us, length us, event | category | flops | bytes accessed | tf_op | source)
XLA Modules:
  0.0 212.2 jit_solution(8542486716324673507)
XLA Ops:
  0.0 210.5 %margins.1 = f32[512,128]{1,0:T(8,128)} custom-call(s32[2]{0:T(128)} %slot_hbm.1, s32[2]{0:T(128)} %shift_hbm.1, bf16[2,2,512,2048]{3,2,1,0:T(8,128)(2,1)} %bands.1), custom_call_target="tpu_custom_call" | custom-call | tf_op jit(solution)/shard_map/margins/pallas_call | solution.py:333
  210.6 1.7 copy.6
